TPU v7x, 32 devices: a whole 2x2x4 slice. The times are simulated.
32 devices in a mesh: dp: 16 (over z, x, core), pair: 2 (over y).
Axes of the slice: x: 2, y: 2, z: 4, core: 2. Of those that a mesh axis runs over, the one named last changes fastest.
Arguments:
- tokens: bfloat16 [65536, 512], P(('dp', 'pair')), may hold values from -12 to 12
- cotangent: bfloat16 [65536, 512], P(('dp', 'pair')), may hold values from -6 to 6
- counts: int32 [128], P(('dp', 'pair')), may hold values from 12 to 64, as said below
- shifts: int32 [128, 2], P(('dp', 'pair')), may hold values from 0 to 3
- qkv_weight: bfloat16 [512, 1536], P(('dp', 'pair')), may hold values from -0.25 to 0.25
- proj_weight: bfloat16 [512, 512], P(('dp', 'pair')), may hold values from -1 to 1
- up_weight: bfloat16 [512, 2048], P(('dp', 'pair')), may hold values from -0.25 to 0.25
- down_weight: bfloat16 [2048, 512], P(('dp', 'pair')), may hold values from -0.1875 to 0.1875
- first_gain: bfloat16 [512], P(('dp', 'pair')), may hold values from 0.099609375 to 1.8984375
- first_bias: bfloat16 [512], P(('dp', 'pair')), may hold values from -3 to 3
- second_gain: bfloat16 [512], P(('dp', 'pair')), may hold values from 0.099609375 to 1.8984375
- second_bias: bfloat16 [512], P(('dp', 'pair')), may hold values from -3 to 3
- query_bias: bfloat16 [512], P(('dp', 'pair')), may hold values from -3 to 3
- value_bias: bfloat16 [512], P(('dp', 'pair')), may hold values from -3 to 3
- proj_bias: bfloat16 [512], P(('dp', 'pair')), may hold values from -3 to 3
- up_bias: bfloat16 [2048], P(('dp', 'pair')), may hold values from -3 to 3
- down_bias: bfloat16 [512], P(('dp', 'pair')), may hold values from -3 to 3
- rel_table: bfloat16 [49, 16], replicated, may hold values from -6 to 6
Outputs:
- out: bfloat16 [65536, 512], P(('dp', 'pair'))
- grad_tokens: float32 [65536, 512], P(('dp', 'pair'))
- grad_qkv_weight: float32 [512, 1536], P(('dp', 'pair'))
- grad_proj_weight: float32 [512, 512], P(('dp', 'pair'))
- grad_up_weight: float32 [512, 2048], P(('dp', 'pair'))
- grad_down_weight: float32 [2048, 512], P(('dp', 'pair'))
- grad_first_gain: float32 [512], P(('dp', 'pair'))
- grad_first_bias: float32 [512], P(('dp', 'pair'))
- grad_second_gain: float32 [512], P(('dp', 'pair'))
- grad_second_bias: float32 [512], P(('dp', 'pair'))
- grad_query_bias: float32 [512], P(('dp', 'pair'))
- grad_value_bias: float32 [512], P(('dp', 'pair'))
- grad_proj_bias: float32 [512], P(('dp', 'pair'))
- grad_up_bias: float32 [2048], P(('dp', 'pair'))
- grad_down_bias: float32 [512], P(('dp', 'pair'))
- grad_rel_table: float32 [49, 16], replicated
Inputs may be any that keep to these rules, and one draw needn't show every extreme that they name: `counts`: patch rows at or beyond a clip's count are padding; some clip has all 64 rows visible.
All inputs are finite; a program needn't handle non-finite values.
Results may differ from a plain program's by a relative error of at most 0.014.
Values may be sent and summed in bfloat16 or wider, within the bound.
No kernel may reach another device: no remote copies, remote signals or barrier semaphores. Data moves between devices by JAX's collectives and lax.ppermute only.
A program may use at most 192 MiB of HBM per device.

v0:
```python
import jax
import jax.numpy as jnp
from jax import lax
from jax.sharding import PartitionSpec as P

HEADS = 16
GRID_T = 64
GRID_F = 8
WIN = 4


EPS = 1e-06
HIGH = lax.Precision.HIGHEST
NEGATIVE = -1e30


def block_layout(shift_pair, visible_rows):
    band_rows = min(16, GRID_T)
    position = jnp.arange(GRID_T * GRID_F, dtype=jnp.int32)
    rolled_t = position // GRID_F
    column = position % GRID_F
    rolled_f = (column - shift_pair[1]) % GRID_F
    band = rolled_t % band_rows // WIN
    wrap_t = (rolled_t + shift_pair[0] >= GRID_T).astype(jnp.int32)
    wrap_f = (column < shift_pair[1]).astype(jnp.int32)
    group_id = (band * (GRID_F // WIN) + rolled_f // WIN) * 4 + wrap_t * 2 + wrap_f
    visible = (rolled_t + shift_pair[0]) % GRID_T < visible_rows
    inner_a = rolled_t % WIN
    inner_b = rolled_f % WIN
    return (group_id, visible, inner_a, inner_b)


def roll_clips(clip_rows, starts):
    doubled = jnp.concatenate([clip_rows, clip_rows], 1)
    length = clip_rows.shape[1]
    return jax.vmap(lambda single, begin: lax.dynamic_slice_in_dim(single, begin, length, 0))(
        doubled, starts
    )


def norm_stats(values):
    row_mean = jnp.mean(values, -1, keepdims=True)
    centred = values - row_mean
    inv_std = lax.rsqrt(jnp.mean(centred * centred, -1, keepdims=True) + EPS)
    return (centred * inv_std, inv_std)


def norm_back(grad_out, normed, inv_std, gain):
    grad_normed = grad_out * gain
    return inv_std * (
        grad_normed
        - jnp.mean(grad_normed, -1, keepdims=True)
        - normed * jnp.mean(grad_normed * normed, -1, keepdims=True)
    )


def fetch(
    qkv_weight,
    proj_weight,
    up_weight,
    down_weight,
    first_gain,
    first_bias,
    second_gain,
    second_bias,
    query_bias,
    value_bias,
    proj_bias,
    up_bias,
    down_bias,
):
    paired = (
        lax.all_gather(qkv_weight, "pair", axis=0, tiled=True),
        lax.all_gather(proj_weight, "pair", axis=0, tiled=True),
        lax.all_gather(up_weight, "pair", axis=0, tiled=True),
        lax.all_gather(down_weight, "pair", axis=0, tiled=True),
        lax.all_gather(first_gain, "pair", axis=0, tiled=True),
        lax.all_gather(first_bias, "pair", axis=0, tiled=True),
        lax.all_gather(second_gain, "pair", axis=0, tiled=True),
        lax.all_gather(second_bias, "pair", axis=0, tiled=True),
        lax.all_gather(query_bias, "pair", axis=0, tiled=True),
        lax.all_gather(value_bias, "pair", axis=0, tiled=True),
        lax.all_gather(proj_bias, "pair", axis=0, tiled=True),
        lax.all_gather(up_bias, "pair", axis=0, tiled=True),
        lax.all_gather(down_bias, "pair", axis=0, tiled=True),
    )
    fetched = (
        lax.all_gather(paired[0], "dp", axis=0, tiled=True),
        lax.all_gather(paired[1], "dp", axis=0, tiled=True),
        lax.all_gather(paired[2], "dp", axis=0, tiled=True),
        lax.all_gather(paired[3], "dp", axis=0, tiled=True),
        lax.all_gather(paired[4], "dp", axis=0, tiled=True),
        lax.all_gather(paired[5], "dp", axis=0, tiled=True),
        lax.all_gather(paired[6], "dp", axis=0, tiled=True),
        lax.all_gather(paired[7], "dp", axis=0, tiled=True),
        lax.all_gather(paired[8], "dp", axis=0, tiled=True),
        lax.all_gather(paired[9], "dp", axis=0, tiled=True),
        lax.all_gather(paired[10], "dp", axis=0, tiled=True),
        lax.all_gather(paired[11], "dp", axis=0, tiled=True),
        lax.all_gather(paired[12], "dp", axis=0, tiled=True),
    )
    return fetched


def settle(grads):
    half_sums = (
        lax.psum_scatter(grads[0], "dp", scatter_dimension=0, tiled=True),
        lax.psum_scatter(grads[1], "dp", scatter_dimension=0, tiled=True),
        lax.psum_scatter(grads[2], "dp", scatter_dimension=0, tiled=True),
        lax.psum_scatter(grads[3], "dp", scatter_dimension=0, tiled=True),
        lax.psum_scatter(grads[4], "dp", scatter_dimension=0, tiled=True),
        lax.psum_scatter(grads[5], "dp", scatter_dimension=0, tiled=True),
        lax.psum_scatter(grads[6], "dp", scatter_dimension=0, tiled=True),
        lax.psum_scatter(grads[7], "dp", scatter_dimension=0, tiled=True),
        lax.psum_scatter(grads[8], "dp", scatter_dimension=0, tiled=True),
        lax.psum_scatter(grads[9], "dp", scatter_dimension=0, tiled=True),
        lax.psum_scatter(grads[10], "dp", scatter_dimension=0, tiled=True),
        lax.psum_scatter(grads[11], "dp", scatter_dimension=0, tiled=True),
        lax.psum_scatter(grads[12], "dp", scatter_dimension=0, tiled=True),
    )
    shares = (
        lax.psum_scatter(
            half_sums[0].astype(jnp.bfloat16), "pair", scatter_dimension=0, tiled=True
        ).astype(jnp.float32),
        lax.psum_scatter(
            half_sums[1].astype(jnp.bfloat16), "pair", scatter_dimension=0, tiled=True
        ).astype(jnp.float32),
        lax.psum_scatter(
            half_sums[2].astype(jnp.bfloat16), "pair", scatter_dimension=0, tiled=True
        ).astype(jnp.float32),
        lax.psum_scatter(
            half_sums[3].astype(jnp.bfloat16), "pair", scatter_dimension=0, tiled=True
        ).astype(jnp.float32),
        lax.psum_scatter(
            half_sums[4].astype(jnp.bfloat16), "pair", scatter_dimension=0, tiled=True
        ).astype(jnp.float32),
        lax.psum_scatter(
            half_sums[5].astype(jnp.bfloat16), "pair", scatter_dimension=0, tiled=True
        ).astype(jnp.float32),
        lax.psum_scatter(
            half_sums[6].astype(jnp.bfloat16), "pair", scatter_dimension=0, tiled=True
        ).astype(jnp.float32),
        lax.psum_scatter(
            half_sums[7].astype(jnp.bfloat16), "pair", scatter_dimension=0, tiled=True
        ).astype(jnp.float32),
        lax.psum_scatter(
            half_sums[8].astype(jnp.bfloat16), "pair", scatter_dimension=0, tiled=True
        ).astype(jnp.float32),
        lax.psum_scatter(
            half_sums[9].astype(jnp.bfloat16), "pair", scatter_dimension=0, tiled=True
        ).astype(jnp.float32),
        lax.psum_scatter(
            half_sums[10].astype(jnp.bfloat16), "pair", scatter_dimension=0, tiled=True
        ).astype(jnp.float32),
        lax.psum_scatter(
            half_sums[11].astype(jnp.bfloat16), "pair", scatter_dimension=0, tiled=True
        ).astype(jnp.float32),
        lax.psum_scatter(
            half_sums[12].astype(jnp.bfloat16), "pair", scatter_dimension=0, tiled=True
        ).astype(jnp.float32),
    )
    return tuple(shares)


def forward_pass(x_rows, allowed, pos_bias, full):
    qkv_w, proj_w, up_w, down_w = (full[0], full[1], full[2], full[3])
    gain_one = full[4].astype(jnp.float32)
    bias_one = full[5].astype(jnp.float32)
    gain_two = full[6].astype(jnp.float32)
    bias_two = full[7].astype(jnp.float32)
    q_bias = full[8].astype(jnp.float32)
    v_bias = full[9].astype(jnp.float32)
    p_bias = full[10].astype(jnp.float32)
    u_bias = full[11].astype(jnp.float32)
    d_bias = full[12].astype(jnp.float32)
    width = x_rows.shape[1]
    block_len = allowed.shape[1]
    blocks = x_rows.shape[0] // block_len
    shape_w = (blocks, block_len, HEADS, width // HEADS)
    scale = (width // HEADS) ** (-0.5)
    normed_one, inv_one = norm_stats(x_rows)
    act_one = (normed_one * gain_one + bias_one).astype(jnp.bfloat16)
    qkv_out = jnp.dot(act_one, qkv_w, preferred_element_type=jnp.float32)
    queries = (qkv_out[:, :width] + q_bias).astype(jnp.bfloat16).reshape(shape_w)
    key_rows = qkv_out[:, width : 2 * width].astype(jnp.bfloat16).reshape(shape_w)
    value_rows = (qkv_out[:, 2 * width :] + v_bias).astype(jnp.bfloat16).reshape(shape_w)
    scores = (
        jnp.einsum("wihd,wjhd->whij", queries, key_rows, preferred_element_type=jnp.float32) * scale
        + pos_bias
    )
    mask_b = allowed[:, None]
    masked = jnp.where(mask_b, scores, NEGATIVE)
    row_top = jnp.max(masked, -1, keepdims=True)
    exp_terms = jnp.where(mask_b, jnp.exp(masked - row_top), 0.0)
    prob_f = exp_terms / jnp.sum(exp_terms, -1, keepdims=True)
    prob_low = prob_f.astype(jnp.bfloat16)
    context = jnp.einsum(
        "whij,wjhd->wihd", prob_low, value_rows, preferred_element_type=jnp.float32
    )
    context_low = context.reshape(-1, width).astype(jnp.bfloat16)
    branch = jnp.dot(context_low, proj_w, preferred_element_type=jnp.float32) + p_bias
    mid = x_rows + branch
    normed_two, inv_two = norm_stats(mid)
    act_two = (normed_two * gain_two + bias_two).astype(jnp.bfloat16)
    hidden = jnp.dot(act_two, up_w, preferred_element_type=jnp.float32) + u_bias
    gelu_low = jax.nn.gelu(hidden, approximate=False).astype(jnp.bfloat16)
    output = mid + jnp.dot(gelu_low, down_w, preferred_element_type=jnp.float32) + d_bias
    kept = (
        act_one,
        normed_one,
        inv_one,
        queries,
        key_rows,
        value_rows,
        prob_f,
        prob_low,
        context_low,
        normed_two,
        inv_two,
        act_two,
        hidden,
        gelu_low,
    )
    return (output, kept)


def backward_pass(grad_rows, kept, full):
    (
        act_one,
        normed_one,
        inv_one,
        queries,
        key_rows,
        value_rows,
        prob_f,
        prob_low,
        context_low,
        normed_two,
        inv_two,
        act_two,
        hidden,
        gelu_low,
    ) = kept
    qkv_w, proj_w, up_w, down_w = (full[0], full[1], full[2], full[3])
    gain_one = full[4].astype(jnp.float32)
    gain_two = full[6].astype(jnp.float32)
    width = act_one.shape[1]
    shape_w = queries.shape
    scale = (width // HEADS) ** (-0.5)
    grad_f = grad_rows.astype(jnp.float32)
    g_down_w = jnp.einsum("nf,nd->fd", gelu_low, grad_rows, preferred_element_type=jnp.float32)
    g_down_b = jnp.sum(grad_f, 0)
    g_gelu = jnp.einsum("nd,fd->nf", grad_rows, down_w, preferred_element_type=jnp.float32)
    gelu_value, gelu_pull = jax.vjp(lambda inner_h: jax.nn.gelu(inner_h, approximate=False), hidden)
    g_hidden = gelu_pull(g_gelu)[0].astype(jnp.bfloat16)
    g_up_b = jnp.sum(g_hidden.astype(jnp.float32), 0)
    g_up_w = jnp.einsum("nd,nf->df", act_two, g_hidden, preferred_element_type=jnp.float32)
    g_act_two = jnp.einsum("nf,df->nd", g_hidden, up_w, preferred_element_type=jnp.float32)
    g_gain_two = jnp.sum(g_act_two * normed_two, 0)
    g_bias_two = jnp.sum(g_act_two, 0)
    g_mid = grad_f + norm_back(g_act_two, normed_two, inv_two, gain_two)
    g_branch = g_mid.astype(jnp.bfloat16)
    g_proj_b = jnp.sum(g_branch.astype(jnp.float32), 0)
    g_proj_w = jnp.einsum("nc,nd->cd", context_low, g_branch, preferred_element_type=jnp.float32)
    g_context = (
        jnp.einsum("nd,cd->nc", g_branch, proj_w, preferred_element_type=jnp.float32)
        .astype(jnp.bfloat16)
        .reshape(shape_w)
    )
    g_prob = jnp.einsum(
        "wihd,wjhd->whij", g_context, value_rows, preferred_element_type=jnp.float32
    )
    g_value = jnp.einsum("whij,wihd->wjhd", prob_low, g_context, preferred_element_type=jnp.float32)
    g_scores = (prob_f * (g_prob - jnp.sum(prob_f * g_prob, -1, keepdims=True))).astype(
        jnp.bfloat16
    )
    g_query = (
        jnp.einsum("whij,wjhd->wihd", g_scores, key_rows, preferred_element_type=jnp.float32)
        * scale
    )
    g_key = (
        jnp.einsum("whij,wihd->wjhd", g_scores, queries, preferred_element_type=jnp.float32) * scale
    )
    g_qkv = jnp.concatenate(
        [g_query.reshape(-1, width), g_key.reshape(-1, width), g_value.reshape(-1, width)], 1
    ).astype(jnp.bfloat16)
    g_q_b = jnp.sum(g_qkv[:, :width].astype(jnp.float32), 0)
    g_v_b = jnp.sum(g_qkv[:, 2 * width :].astype(jnp.float32), 0)
    g_qkv_w = jnp.einsum("nd,nc->dc", act_one, g_qkv, preferred_element_type=jnp.float32)
    g_act_one = jnp.einsum("nc,dc->nd", g_qkv, qkv_w, preferred_element_type=jnp.float32)
    g_gain_one = jnp.sum(g_act_one * normed_one, 0)
    g_bias_one = jnp.sum(g_act_one, 0)
    g_input = g_mid + norm_back(g_act_one, normed_one, inv_one, gain_one)
    grads = (
        g_qkv_w,
        g_proj_w,
        g_up_w,
        g_down_w,
        g_gain_one,
        g_bias_one,
        g_gain_two,
        g_bias_two,
        g_q_b,
        g_v_b,
        g_proj_b,
        g_up_b,
        g_down_b,
    )
    return (grads, g_scores, g_input)


def on_device(
    tokens,
    cotangent,
    counts,
    shifts,
    qkv_weight,
    proj_weight,
    up_weight,
    down_weight,
    first_gain,
    first_bias,
    second_gain,
    second_bias,
    query_bias,
    value_bias,
    proj_bias,
    up_bias,
    down_bias,
    rel_table,
):
    patches = GRID_T * GRID_F
    clip_count = counts.shape[0]
    width = tokens.shape[1]
    block_len = min(16, GRID_T) * GRID_F
    per_clip = patches // block_len
    rel_count = rel_table.shape[0]
    group_id, visible, inner_a, inner_b = jax.vmap(block_layout)(shifts, counts)
    group_b = group_id.reshape(-1, block_len)
    visible_b = visible.reshape(-1, block_len)
    diagonal_on = jnp.eye(block_len, dtype=bool)
    allowed = (group_b[:, :, None] == group_b[:, None, :]) & (
        visible_b[:, None, :] | diagonal_on[None]
    )
    first_a = inner_a[:, :block_len]
    first_b = inner_b[:, :block_len]
    codes = (first_a[:, :, None] - first_a[:, None, :] + WIN - 1) * (2 * WIN - 1) + (
        first_b[:, :, None] - first_b[:, None, :] + WIN - 1
    )
    onehot = (
        codes.reshape(clip_count, -1)[:, :, None]
        == jnp.arange(rel_count, dtype=jnp.int32)[None, None, :]
    ).astype(jnp.float32)
    clip_bias = jnp.einsum(
        "cpe,eh->chp", onehot, rel_table.astype(jnp.float32), precision=HIGH
    ).reshape(clip_count, -1, block_len, block_len)
    pos_bias = jnp.repeat(clip_bias, per_clip, axis=0)
    starts_in = shifts[:, 0] * GRID_F
    starts_out = (GRID_T - shifts[:, 0]) % GRID_T * GRID_F
    x_rows = (
        roll_clips(tokens.reshape(clip_count, patches, width), starts_in)
        .reshape(-1, width)
        .astype(jnp.float32)
    )
    grad_rows = roll_clips(cotangent.reshape(clip_count, patches, width), starts_in).reshape(
        -1, width
    )
    full = fetch(
        qkv_weight,
        proj_weight,
        up_weight,
        down_weight,
        first_gain,
        first_bias,
        second_gain,
        second_bias,
        query_bias,
        value_bias,
        proj_bias,
        up_bias,
        down_bias,
    )
    output, kept = forward_pass(x_rows, allowed, pos_bias, full)
    back_full = fetch(
        qkv_weight,
        proj_weight,
        up_weight,
        down_weight,
        first_gain,
        first_bias,
        second_gain,
        second_bias,
        query_bias,
        value_bias,
        proj_bias,
        up_bias,
        down_bias,
    )
    unused_out, back_kept = forward_pass(x_rows, allowed, pos_bias, back_full)
    grads, g_scores, g_input = backward_pass(grad_rows, back_kept, back_full)
    shares = settle(grads)
    heads_n = g_scores.shape[1]
    g_pos = jnp.sum(
        g_scores.astype(jnp.float32).reshape(clip_count, per_clip, heads_n, block_len * block_len),
        1,
    )
    table_term = jnp.einsum("cpe,chp->eh", onehot, g_pos, precision=HIGH)
    table_total = lax.psum(table_term, ("dp", "pair"))
    out_rows = (
        roll_clips(output.reshape(clip_count, patches, width), starts_out)
        .reshape(-1, width)
        .astype(jnp.bfloat16)
    )
    grad_tokens = roll_clips(g_input.reshape(clip_count, patches, width), starts_out).reshape(
        -1, width
    )
    return (out_rows, grad_tokens) + shares + (table_total,)


def solution(mesh):
    in_specs = (
        P(("dp", "pair"), None),
        P(("dp", "pair"), None),
        P(("dp", "pair")),
        P(("dp", "pair"), None),
        P(("dp", "pair"), None),
        P(("dp", "pair"), None),
        P(("dp", "pair"), None),
        P(("dp", "pair"), None),
        P(("dp", "pair")),
        P(("dp", "pair")),
        P(("dp", "pair")),
        P(("dp", "pair")),
        P(("dp", "pair")),
        P(("dp", "pair")),
        P(("dp", "pair")),
        P(("dp", "pair")),
        P(("dp", "pair")),
        P(),
    )
    out_specs = (
        P(("dp", "pair"), None),
        P(("dp", "pair"), None),
        P(("dp", "pair"), None),
        P(("dp", "pair"), None),
        P(("dp", "pair"), None),
        P(("dp", "pair"), None),
        P(("dp", "pair")),
        P(("dp", "pair")),
        P(("dp", "pair")),
        P(("dp", "pair")),
        P(("dp", "pair")),
        P(("dp", "pair")),
        P(("dp", "pair")),
        P(("dp", "pair")),
        P(("dp", "pair")),
        P(),
    )
    return jax.shard_map(
        on_device, mesh=mesh, in_specs=in_specs, out_specs=out_specs, check_vma=False
    )
```

profile of v0, /device:TPU:0, one launch (start us, length us, event | category | flops | bytes accessed | tf_op | source)
XLA Modules:
  0.0 728.0 jit_solution(9092817557586355054)
XLA Ops:
  7.2 7.4 %all_gather.106 = bf16[32,1536]{1,0:T(8,128)(2,1)} all-gather(bf16[16,1536]{1,0:T(8,128)(2,1)} %param.22), channel_id=1, replica_groups=mesh['dp'=16,'pair'=2] {'pair'}, dimensions={0}, use_global_device_ids=true | all-gather | bytes 147456 | tf_op jit(solution)/shard_map/all_gather | solution.py:73
  14.7 5.3 all_gather.120
  20.1 6.1 all_gather.124
  38.3 5.0 all-reduce.40
  45.0 31.0 %all-reduce.38 = (bf16[512]{0:T(512)(128)(2,1)S(1)}, bf16[512]{0:T(512)(128)(2,1)S(1)}, bf16[512]{0:T(512)(128)(2,1)S(1)}, bf16[512]{0:T(512)(128)(2,1)S(1)}, bf...) all-reduce(bf16[512]{0:T(512)(128)(2,1)S(1)} %dynamic-update-slice., ...), channel_id=1, replica_groups=mesh['dp'=16,'pair'=2] {'dp'}, use_global_device_ids=true, to_apply=%add.11 | all-reduce | flops 4096 | bytes 16384
  76.1 4.5 pad_maximum_fusion.2
  81.5 12.3 %while.8 = (s32[]{:T(128)}, bf16[4,1024,512]{2,1,0:T(8,128)(2,1)}, s32[4,3]{1,0:T(4,128)S(1)}, bf16[4,512,512]{2,1,0:T(8,128)(2,1)S(1)}) while((s32[]{:T(128)}, bf16[4,1024,512]{2,1,0:T(8,128)(2,1)}, s32[4,3]{1,0:T(4,128)S(1)}, bf16[4,512,512]{2,1,0:T(8,128)(2,1)S(1)}) %tuple.106), condition=%wide.while_cond.clone, body=%wide.while_body.sunk.clone | while | flops 2 | bytes 1048685 | solution.py:36
  101.7 5.4 copy.77
  107.1 4.4 all_gather.112
  111.5 19.6 %all_gather.113 = bf16[512,512]{1,0:T(8,128)(2,1)S(1)} all-gather(bf16[32,512]{1,0:T(8,128)(2,1)S(1)} %all_gather.112), channel_id=1, replica_groups=mesh['dp'=16,'pair'=2] {'dp'}, dimensions={0}, use_global_device_ids=true | all-gather | bytes 557056 | tf_op jit(solution)/shard_map/all_gather | solution.py:89
  131.0 19.3 %all-gather = bf16[16,1,128]{2,1,0:T(2,128)(2,1)S(1)} all-gather(bf16[1,1,128]{2,1,0:T(2,128)(2,1)S(1)} %bitcast.231), channel_id=1, replica_groups=mesh['dp'=16,'pair'=2] {'dp'}, dimensions={0}, use_global_device_ids=true | all-gather | bytes 4352 | tf_op jit(solution)/shard_map/all_gather | solution.py:99
  150.3 4.5 pad_maximum_fusion.3
  156.4 15.5 %while.10 = (s32[]{:T(128)}, bf16[4,1024,512]{2,1,0:T(8,128)(2,1)}, s32[4,3]{1,0:T(4,128)S(1)}, bf16[4,512,512]{2,1,0:T(8,128)(2,1)}) while((s32[]{:T(128)}, bf16[4,1024,512]{2,1,0:T(8,128)(2,1)}, s32[4,3]{1,0:T(4,128)S(1)}, bf16[4,512,512]{2,1,0:T(8,128)(2,1)}) %tuple.142), condition=%wide.while_cond.2.clone, body=%wide.while_body.2.sunk.clone | while | flops 2 | bytes 1050209 | solution.py:36
  174.7 5.5 fusion.102
  185.1 4.0 copy.73
  189.1 3.7 copy.103
  192.8 3.9 copy.74
  200.4 9.6 %fusion.2 = f32[16,16,128,128]{2,3,1,0:T(8,128)} fusion(f32[4,16,128,128]{2,3,1,0:T(8,128)} %copy.77, pred[16,128,128]{1,2,0:T(8,128)(4,1)S(1)} %or_and_fusion, bf16[16,128,16,32]{1,0,3,2:T(8,128)(2,1)S(1)} %bitcast.191, bf16[16,128,16,32]{1,0,3,2:T(8,128)(2,1)S(1)} %bitcast.193), kind=kOutput, calls=%fused_computation.12 | convolution fusion | flops 281018368 | bytes 25427968 | tf_op jit(solution)/shard_map/wihd,wjhd->whij/dot_general | solution.py:188
  210.0 17.6 %fusion.100 = (f32[16,16,128]{2,1,0:T(8,128)S(1)}, f32[16,16,128,128]{2,3,1,0:T(8,128)}) fusion(f32[16,16,128,128]{2,3,1,0:T(8,128)} %fusion.2, pred[16,128,128]{1,2,0:T(8,128)(4,1)S(1)} %or_and_fusion), kind=kOutput, calls=%fused_computation.229 | output fusion | flops 12583039 | bytes 33947648 | tf_op jit(solution)/shard_map/sub | solution.py:194
  227.6 4.1 copy.72
  233.9 8.8 %convert_bitcast_fusion.1 = bf16[16,128,16,32]{1,3,2,0:T(8,128)(2,1)S(1)} fusion(bf16[16,128,16,32]{1,0,3,2:T(8,128)(2,1)S(1)} %bitcast.215, f32[16,16,128,128]{2,3,1,0:T(8,128)} %get-tuple-element.151, f32[16,16,128]{2,1,0:T(8,128)S(1)} %get-tuple-element.150), kind=kOutput, calls=%fused_computation.92 | convolution fusion | flops 277872640 | bytes 21102592 | tf_op jit(solution)/shard_map/whij,wjhd->wihd/dot_general | solution.py:197
  248.7 44.9 %multiply_convert_fusion.1 = (bf16[2048,2048]{1,0:T(8,128)(2,1)}, f32[2048,2048]{1,0:T(8,128)}, f32[2048,2048]{1,0:T(8,128)}) fusion(f32[2048]{0:T(1024)S(1)} %bitcast.229, bf16[512,2048]{1,0:T(8,128)(2,1)} %all-gather.7.cloned.1.call-done, f32[2048,512]{1,0:T(8,128)} %copy-done.15, f32[512]{0:T(512)S(1)} %convert_element_type.230, ...), kind=kOutput, calls=%fused_computation.17 | convolution fusion | flops 4577034240 | bytes 48263168 | tf_op jit(solution)/shard_map/dot_general | solution.py:205
  293.5 19.7 %convert_reduce_fusion = (f32[2048]{0:T(1024)S(1)}, bf16[2048,2048]{1,0:T(8,128)(2,1)}) fusion(f32[2048,2048]{1,0:T(8,128)} %get-tuple-element.126, bf16[2048,512]{1,0:T(8,128)(2,1)S(1)} %bitcast.200, bf16[2048,512]{1,0:T(8,128)(2,1)} %all-gather.9.cloned.1.call-done, f32[2048,2048]{1,0:T(8,128)} %get-tuple-element.154, f32[2048]{0:T(1024)S(1)} %bitcast.230), kind=kOutput, calls=%fused_computation.13 | convolution fusion | flops 4366268416 | bytes 46153728 | tf_op jit(solution)/shard_map/nd,fd->nf/dot_general | solution.py:253
  313.2 10.7 %multiply_reduce_fusion.1 = (f32[512]{0:T(512)S(1)}, f32[2048]{0:T(1024)S(1)}, f32[2048]{0:T(1024)S(1)}, f32[512]{0:T(512)S(1)}, f32[2048,512]{1,0:T(8,128)S(1)}) fusion(f32[2048,512]{1,0:T(8,128)} %copy-done.15, f32[2048]{0:T(1024)S(1)} %add_rsqrt_fusion, f32[2048]{0:T(1024)S(1)} %broadcast_multiply_fusion.4, f32[512]{0:T(512)S(1)} %convert_element_type.229, ...), kind=kOutput, calls=%fused_computation.69 | convolution fusion | flops 4304399360 | bytes 18913280 | tf_op jit(solution)/shard_map/nf,df->nd/dot_general | solution.py:258
  330.8 4.0 copy.81
  338.3 11.8 %convert_bitcast_fusion = bf16[16,128,16,32]{1,3,2,0:T(8,128)(2,1)} fusion(bf16[16,128,16,32]{1,0,3,2:T(8,128)(2,1)S(1)} %bitcast.217, f32[16,16,128,128]{2,3,1,0:T(8,128)} %get-tuple-element.151, f32[16,16,128]{2,1,0:T(8,128)S(1)} %copy-done.31), kind=kOutput, calls=%fused_computation.91 | convolution fusion | flops 277872640 | bytes 21102592 | tf_op jit(solution)/shard_map/whij,wihd->wjhd/dot_general | solution.py:273
  350.1 12.1 %multiply_reduce_fusion = (f32[16,16,128]{2,1,0:T(8,128)S(1)}, f32[16,16,128,128]{2,3,1,0:T(8,128)}) fusion(f32[16,16,128,128]{2,3,1,0:T(8,128)} %get-tuple-element.151, f32[16,16,128]{2,1,0:T(8,128)S(1)} %copy-done.31, bf16[16,128,16,32]{1,0,3,2:T(8,128)(2,1)S(1)} %bitcast.216, bf16[16,128,16,32]{1,0,3,2:T(8,128)(2,1)} %bitcast.218), kind=kOutput, calls=%fused_computation.15 | convolution fusion | flops 280985600 | bytes 38010880 | tf_op jit(solution)/shard_map/wihd,wjhd->whij/dot_general | solution.py:270
  362.1 12.3 %multiply_convert_fusion = bf16[16,16,128,128]{2,3,1,0:T(8,128)(2,1)S(1)} fusion(f32[16,16,128,128]{2,3,1,0:T(8,128)} %get-tuple-element.157, f32[16,16,128]{2,1,0:T(8,128)S(1)} %get-tuple-element.156, f32[16,16,128,128]{2,3,1,0:T(8,128)} %get-tuple-element.151, f32[16,16,128]{2,1,0:T(8,128)S(1)} %copy-done.31), kind=kLoop, calls=%fused_computation.14 | loop fusion | flops 16777216 | bytes 42205184 | tf_op jit(solution)/shard_map/convert_element_type | solution.py:274
  374.5 5.7 fusion.53
  385.9 4.4 copy.89
  403.2 8.1 %fusion.103 = f32[512,1536]{1,0:T(8,128)} fusion(bf16[2048,512]{1,0:T(8,128)(2,1)S(1)} %copy-done.19, bf16[2048,1536]{0,1:T(8,128)(2,1)} %bitcast_dynamic-update-slice_fusion), kind=kOutput, calls=%fused_computation.233 | convolution fusion | flops 3221225472 | bytes 11534336 | tf_op jit(solution)/shard_map/nd,nc->dc/dot_general | solution.py:289
  411.4 11.4 %fusion.91 = f32[512,2048]{1,0:T(8,128)} fusion(bf16[2048,2048]{1,0:T(8,128)(2,1)} %get-tuple-element.160, f32[2048,512]{1,0:T(8,128)} %copy-done.15, f32[512]{0:T(512)S(1)} %convert_element_type.230, f32[512]{0:T(512)S(1)} %convert_element_type.229, f32[2048]{0:T(1024)S(1)} %add_rsqrt_fusion, f32[2048]{0:T(1024)S(1)} %broadcast_multiply_fusion.4), kind=kOutput, calls=%fused_computation.221 | convolution fusion | flops 4300210176 | bytes 16797696 | tf_op jit(solution)/shard_map/nd,nf->df/dot_general | solution.py:257
  427.5 13.0 %copy.93 = f32[16,16,128,128]{3,2,1,0:T(8,128)} copy(bf16[16,16,128,128]{2,3,1,0:T(8,128)(2,1)} %copy-done.2) | data formatting | bytes 25165824 | tf_op jit(solution)/shard_map/reshape | solution.py:404
  444.7 8.3 %fusion.27 = (f32[512]{0:T(512)S(1)}, f32[2048]{0:T(1024)S(1)}, f32[2048]{0:T(1024)S(1)}, f32[512]{0:T(512)S(1)}, f32[2048,512]{1,0:T(8,128)}) fusion(bf16[4,512,512]{2,1,0:T(8,128)(2,1)S(1)} %copy-done.4, f32[2048]{0:T(1024)S(1)} %bitcast.220, f32[2048]{0:T(1024)S(1)} %bitcast.223, f32[512]{0:T(512)S(1)} %copy-done.37, ...), kind=kOutput, calls=%fused_computation.64 | convolution fusion | flops 3231706112 | bytes 14194688 | tf_op jit(solution)/shard_map/nc,dc->nd/dot_general | solution.py:290
  452.9 58.3 %all-reduce.37 = (bf16[512]{0:T(512)(128)(2,1)S(1)}, bf16[512]{0:T(512)(128)(2,1)S(1)}, bf16[512]{0:T(512)(128)(2,1)S(1)}, bf16[512]{0:T(512)(128)(2,1)S(1)}, bf...) all-reduce(f32[512]{0:T(512)S(1)} %get-tuple-element.50, ...), channel_id=10, replica_groups=mesh['dp'=16,'pair'=2] {'dp'}, use_global_device_ids=true, to_apply=%region_20.21.clone | all-reduce | flops 6144 | bytes 36864
  511.8 18.3 %reshape.624 = f32[4,4,16,16384]{3,2,1,0:T(8,128)} reshape(f32[16,16,128,128]{3,2,1,0:T(8,128)} %copy.93) | data formatting | bytes 33554432 | tf_op jit(solution)/shard_map/reshape | solution.py:404
  530.2 10.1 %reduce_sum.219 = f32[4,16,16384]{2,1,0:T(8,128)} reduce(f32[4,4,16,16384]{3,2,1,0:T(8,128)} %reshape.624, f32[]{:T(128)} %constant.171.clone.1), dimensions={1}, to_apply=%region_46.47 | reduce | flops 3145728 | bytes 20971524 | tf_op jit(solution)/shard_map/reduce_sum | solution.py:403
  540.3 10.6 %fusion.104 = f32[2048,512]{1,0:T(8,128)} fusion(bf16[2048,2048]{1,0:T(8,128)(2,1)} %get-tuple-element.125, bf16[2048,512]{1,0:T(8,128)(2,1)} %bitcast.199), kind=kOutput, calls=%fused_computation.234 | convolution fusion | flops 4294967296 | bytes 14680064 | tf_op jit(solution)/shard_map/nf,nd->fd/dot_general | solution.py:251
  551.0 5.3 all-reduce.39
  558.0 9.9 %add_add_fusion = bf16[2048,512]{1,0:T(8,128)(2,1)S(1)} fusion(f32[2048,512]{1,0:T(8,128)} %copy-done.15, bf16[2048,2048]{1,0:T(8,128)(2,1)} %get-tuple-element.125, bf16[2048,512]{1,0:T(8,128)(2,1)} %all-gather.9.cloned.1.call-done, f32[512]{0:T(512)S(1)} %convert_element_type.234), kind=kOutput, calls=%fused_computation.74 | convolution fusion | flops 4298113024 | bytes 16779264 | tf_op jit(solution)/shard_map/dot_general | solution.py:207
  573.5 4.6 pad_maximum_fusion.1
  578.0 15.4 %while.9 = (s32[]{:T(128)}, bf16[4,1024,512]{2,1,0:T(8,128)(2,1)}, s32[4,3]{1,0:T(4,128)S(1)}, bf16[4,512,512]{2,1,0:T(8,128)(2,1)}) while((s32[]{:T(128)}, bf16[4,1024,512]{2,1,0:T(8,128)(2,1)}, s32[4,3]{1,0:T(4,128)S(1)}, bf16[4,512,512]{2,1,0:T(8,128)(2,1)}) %tuple.140), condition=%wide.while_cond.1.clone, body=%wide.while_body.1.sunk.clone | while | flops 2 | bytes 1050209 | solution.py:36
  593.5 17.0 %while.11 = (s32[]{:T(128)}, f32[4,1024,512]{2,1,0:T(8,128)}, s32[4,3]{1,0:T(4,128)S(1)}, f32[4,512,512]{2,1,0:T(8,128)}) while((s32[]{:T(128)}, f32[4,1024,512]{2,1,0:T(8,128)}, s32[4,3]{1,0:T(4,128)S(1)}, f32[4,512,512]{2,1,0:T(8,128)}) %tuple.141), condition=%wide.while_cond.3.clone, body=%wide.while_body.3.sunk.clone | while | flops 2 | bytes 2098785 | solution.py:36
  602.5 3.7 dynamic-slice_dynamic-update-slice_fusion.15
  606.8 3.7 dynamic-slice_dynamic-update-slice_fusion.15
  617.2 8.9 %fusion.56 = f32[49,16]{0,1:T(8,128)S(1)} fusion(f32[4,16,16384]{2,1,0:T(8,128)} %reduce_sum.219, s32[4,16384]{1,0:T(4,128)S(1)} %copy-done.29), kind=kOutput, calls=%fused_computation.106 | convolution fusion | flops 619773952 | bytes 4459584 | tf_op jit(solution)/shard_map/cpe,chp->eh/dot_general | solution.py:407
  626.1 43.3 %reduce-scatter.21.cloned.1.call-done = f32[128,512]{1,0:T(8,128)} async-done(((f32[2048,512]{1,0:T(8,128)}), f32[128,512]{1,0:T(8,128)}) %reduce-scatter.21.cloned.1.call-update) | async-done | bytes 262160 | tf_op jit(solution)/shard_map/reduce_scatter | solution.py:110
  671.6 39.6 %psum.7 = f32[49,16]{0,1:T(8,128)} all-reduce(f32[49,16]{0,1:T(8,128)S(1)} %fusion.56), channel_id=1, replica_groups=mesh['dp'=16,'pair'=2] {'dp','pair'}, use_global_device_ids=true, to_apply=%region_47.48 | all-reduce | flops 784 | bytes 6272 | tf_op jit(solution)/shard_map/psum | solution.py:408
  (305 shorter events, 156.2 us)
Async XLA Ops:
  7.2 89.1 %copy-start = (bf16[49,16]{0,1:T(8,128)(2,1)S(1)}, bf16[49,16]{0,1:T(8,128)(2,1)}, u32[]{:S(2)}) copy-start(bf16[49,16]{0,1:T(8,128)(2,1)} %param.35) | copy-start | bytes 4708
  7.2 167.5 %all-gather.5.cloned.1.call-start = ((), (), s32[]{:S(2)}) async-start(), calls=%async_computation.8 | async-start | bytes 1671168 | tf_op jit(solution)/shard_map/all_gather | solution.py:88
  14.7 234.0 %all-gather.7.cloned.1.call-start = ((), (), s32[]{:S(2)}) async-start(), calls=%async_computation.9 | async-start | bytes 2228224 | tf_op jit(solution)/shard_map/all_gather | solution.py:90
  20.1 273.5 %all-gather.9.cloned.1.call-start = ((), (), s32[]{:S(2)}) async-start(), calls=%async_computation.10 | async-start | bytes 2228224 | tf_op jit(solution)/shard_map/all_gather | solution.py:91
  26.2 584.3 %reduce-scatter.13.cloned.1.call-start = ((), (), s32[]{:S(2)}) async-start(), calls=%async_computation.13 | async-start | bytes 1114112 | tf_op jit(solution)/shard_map/reduce_scatter | solution.py:108
  76.0 96.8 %copy-start.36 = (f32[512]{0:T(512)}, f32[512]{0:T(512)S(1)}, u32[]{:S(2)}) copy-start(f32[512]{0:T(512)S(1)} %convert_element_type.216) | copy-start | bytes 6148
  81.5 14.2 %copy-start.41 = (s32[4]{0:T(128)S(1)}, s32[4]{0:T(128)}, u32[]{:S(2)}) copy-start(s32[4]{0:T(128)} %param.20) | copy-start | bytes 52
  93.8 150.3 %copy-start.3 = (bf16[4,512,512]{2,1,0:T(8,128)(2,1)}, bf16[4,512,512]{2,1,0:T(8,128)(2,1)S(1)}, u32[]{:S(2)}) copy-start(bf16[4,512,512]{2,1,0:T(8,128)(2,1)S(1)} %get-tuple-element.23) | copy-start | bytes 6291460
  95.3 77.5 %copy-start.32 = (f32[1,4,4,128]{3,1,2,0:T(4,128)}, f32[1,4,4,128]{3,1,2,0:T(4,128)S(1)}, u32[]{:S(2)}) copy-start(f32[1,4,4,128]{3,1,2,0:T(4,128)S(1)} %copy.101) | copy-start | bytes 24580
  95.3 77.5 %copy-start.34 = (f32[1,4,4,128]{3,1,2,0:T(4,128)}, f32[1,4,4,128]{3,1,2,0:T(4,128)S(1)}, u32[]{:S(2)}) copy-start(f32[1,4,4,128]{3,1,2,0:T(4,128)S(1)} %copy.100) | copy-start | bytes 24580
  96.3 5.4 copy-start.28
  101.7 5.4 copy-start.38
  131.0 113.2 %copy-start.26 = (bf16[512,512]{1,0:T(8,128)(2,1)}, bf16[512,512]{1,0:T(8,128)(2,1)S(1)}, u32[]{:S(2)}) copy-start(bf16[512,512]{1,0:T(8,128)(2,1)S(1)} %all_gather.113) | copy-start | bytes 1572868
  196.7 3.7 copy-start.10
  227.6 6.3 copy-start.30
  233.9 8.9 %copy-start.22 = (bf16[64,8,16,128]{3,2,1,0:T(8,128)(2,1)}, bf16[64,8,16,128]{3,2,1,0:T(8,128)(2,1)S(1)}, u32[]{:S(2)}) copy-start(bf16[64,8,16,128]{3,2,1,0:T(8,128)(2,1)S(1)} %copy.102) | copy-start | bytes 6291460
  248.7 44.9 %copy-start.14 = (bf16[4,512,512]{2,1,0:T(8,128)(2,1)S(1)}, bf16[4,512,512]{2,1,0:T(8,128)(2,1)}, u32[]{:S(2)}) copy-start(bf16[4,512,512]{2,1,0:T(8,128)(2,1)} %get-tuple-element.39) | copy-start | bytes 6291460
  313.2 10.8 %copy-start.16 = (f32[2048,512]{1,0:T(8,128)S(1)}, f32[2048,512]{1,0:T(8,128)}, u32[]{:S(2)}) copy-start(f32[2048,512]{1,0:T(8,128)} %copy-done.15) | copy-start | bytes 12582916
  324.0 4.1 copy-start.27
  326.1 2.0 copy-start.5
  330.8 7.5 %copy-start.31 = (f32[16,16,128]{2,1,0:T(8,128)S(1)}, f32[16,16,128]{2,1,0:T(8,128)}, u32[]{:S(2)}) copy-start(f32[16,16,128]{2,1,0:T(8,128)} %copy-done.30) | copy-start | bytes 393220
  338.3 11.8 %copy-start.23 = (bf16[64,8,16,128]{3,2,1,0:T(8,128)(2,1)S(1)}, bf16[64,8,16,128]{3,2,1,0:T(8,128)(2,1)}, u32[]{:S(2)}) copy-start(bf16[64,8,16,128]{3,2,1,0:T(8,128)(2,1)} %copy-done.22) | copy-start | bytes 6291460
  362.1 12.4 %copy-start.11 = (bf16[64,8,16,128]{3,2,1,0:T(8,128)(2,1)S(1)}, bf16[64,8,16,128]{3,2,1,0:T(8,128)(2,1)}, u32[]{:S(2)}) copy-start(bf16[64,8,16,128]{3,2,1,0:T(8,128)(2,1)} %copy.103) | copy-start | bytes 6291460
  374.5 5.7 copy-start.2
  374.5 5.7 copy-start.9
  380.2 3.4 copy-start.6
  380.2 3.4 copy-start.21
  385.9 4.4 copy-start.17
  394.9 217.8 %reduce-scatter.9.cloned.1.call-start = ((), (), s32[]{:S(2)}) async-start(), calls=%async_computation.11 | async-start | bytes 3342336 | tf_op jit(solution)/shard_map/reduce_scatter | solution.py:107
  395.1 3.6 copy-start.24
  398.7 4.6 copy-start.19
  411.4 204.1 %reduce-scatter.17.cloned.1.call-start = ((), (), s32[]{:S(2)}) async-start(), calls=%async_computation.15 | async-start | bytes 4456448 | tf_op jit(solution)/shard_map/reduce_scatter | solution.py:109
  422.8 2.9 copy-start.40
  422.8 246.6 %reduce-scatter.21.cloned.1.call-start = ((), (), s32[]{:S(2)}) async-start(), calls=%async_computation.17 | async-start | bytes 4456448 | tf_op jit(solution)/shard_map/reduce_scatter | solution.py:110
  440.5 4.1 copy-start.4
  440.5 4.1 copy-start.33
  440.5 4.1 copy-start.35
  440.5 4.1 copy-start.37
  440.5 4.1 copy-start.42
  551.0 161.4 %reduce-scatter.15.cloned.1.call-start = ((), (), s32[]{:S(2)}) async-start(), calls=%async_computation.14 | async-start | bytes 49152 | tf_op jit(solution)/shard_map/reduce_scatter | solution.py:125
  558.0 12.6 %copy-start.18 = (f32[2048,512]{1,0:T(8,128)S(1)}, f32[2048,512]{1,0:T(8,128)}, u32[]{:S(2)}) copy-start(f32[2048,512]{1,0:T(8,128)} %get-tuple-element.158) | copy-start | bytes 12582916
  567.9 3.7 copy-start.7
  573.5 4.6 copy-start.39
  593.5 23.7 %copy-start.29 = (s32[4,16384]{1,0:T(4,128)S(1)}, s32[4,16384]{1,0:T(4,128)}, u32[]{:S(2)}) copy-start(s32[4,16384]{1,0:T(4,128)} %copy-done.28) | copy-start | bytes 786436
  610.5 110.6 %copy-start.1 = (bf16[49,16]{0,1:T(8,128)(2,1)S(1)}, bf16[49,16]{0,1:T(8,128)(2,1)}, u32[]{:S(2)}) copy-start(bf16[49,16]{0,1:T(8,128)(2,1)} %param.35) | copy-start | bytes 4708
  612.0 101.7 %reduce-scatter.11.cloned.1.call-start = ((), (), s32[]{:S(2)}) async-start(), calls=%async_computation.12 | async-start | bytes 147456 | tf_op jit(solution)/shard_map/reduce_scatter | solution.py:122
  614.3 100.9 %reduce-scatter.19.cloned.1.call-start = ((), (), s32[]{:S(2)}) async-start(), calls=%async_computation.16 | async-start | bytes 196608 | tf_op jit(solution)/shard_map/reduce_scatter | solution.py:128
  617.1 102.4 %reduce-scatter.23.cloned.1.call-start = ((), (), s32[]{:S(2)}) async-start(), calls=%async_computation.18 | async-start | bytes 196608 | tf_op jit(solution)/shard_map/reduce_scatter | solution.py:131
  (6 other events, 8.9 us)
Sparse Core Ops, SparseCore 0:
  14.8 40.0 all-gather.4
  57.1 40.1 all-gather.6
  99.4 40.6 all-gather.8
  395.0 53.5 reduce-scatter.12
  452.7 65.4 reduce-scatter.8
  522.5 71.4 reduce-scatter.16
  597.8 71.5 reduce-scatter.20
  672.2 8.8 reduce-scatter.14
  684.0 9.9 reduce-scatter.10
  696.7 10.3 reduce-scatter.18
  709.3 10.1 reduce-scatter.22
where the time goes:
time: 739 us; the launch traced here: 728 us
  blocking collectives  201 us (27%)
  matrix products  198 us (27%)
  local copies, waits for them, and re-layouts  168 us (23%)
  other arithmetic  93 us (13%)
  waiting for transfers between devices  46.4 us (6%)
  between operations  19.6 us (3%)
    unnamed x4, blocking collectives  99.5 us
    gather x48, local copies, waits for them, and re-layouts  60.1 us
    dot_general x1, matrix products, forward_pass(): hidden = jnp.dot(act_two, up_w, preferred_element_type=jnp.float32) + u_bias  44.9 us
    reduce_scatter x1, waiting for transfers between devices, settle(): lax.psum_scatter(grads[3], 'dp', scatter_dimension=0, tiled=True)  43.3 us
    unnamed x143, local copies, waits for them, and re-layouts  42.4 us
    psum x1, blocking collectives, on_device(): table_total = lax.psum(table_term, ('dp', 'pair'))  39.6 us
    reshape x2, local copies, waits for them, and re-layouts, on_device(): g_scores.astype(jnp.float32)  31.3 us
    dot_general x1, matrix products, backward_pass(): jnp.einsum('nd,fd->nf', grad_rows, down_w, preferred_element_type=jnp.flo...  19.7 us
  transfers between devices with their start and end apart: 11, of which 2 were waited for; matrix products, arithmetic and copies ran while one was open for 48% of the time, Pallas kernels for 0%

commit v1 on v0

v1 whole, which is shorter than its diff:
```python
import functools

import jax
import jax.numpy as jnp
import numpy as np
from jax import lax
from jax.experimental import pallas as pl
from jax.experimental.pallas import tpu as pltpu
from jax.sharding import PartitionSpec as P

HEADS = 16
GRID_T = 64
GRID_F = 8
WIN = 4
PLACES = WIN * WIN
PATCHES = GRID_T * GRID_F
BLOCK = 64
BLOCKS = PATCHES // BLOCK
AXES = ("dp", "pair")

EPS = 1e-06
HIGH = lax.Precision.HIGHEST
NEGATIVE = -1e30
F32 = jnp.float32
BF16 = jnp.bfloat16
VMEM_BYTES = 60 * 1024 * 1024
ROWS = 32


def dot_nn(a, b):
    return lax.dot_general(a, b, (((1,), (0,)), ((), ())), preferred_element_type=F32)


def dot_nt(a, b):
    return lax.dot_general(a, b, (((1,), (1,)), ((), ())), preferred_element_type=F32)


def dot_tn(a, b):
    return lax.dot_general(a, b, (((0,), (0,)), ((), ())), preferred_element_type=F32)


def norm_stats(values):
    row_mean = jnp.mean(values, -1, keepdims=True)
    centred = values - row_mean
    inv_std = lax.rsqrt(jnp.mean(centred * centred, -1, keepdims=True) + EPS)
    return centred * inv_std, inv_std


def norm_back(grad_out, normed, inv_std, gain):
    grad_normed = grad_out * gain
    return inv_std * (
        grad_normed
        - jnp.mean(grad_normed, -1, keepdims=True)
        - normed * jnp.mean(grad_normed * normed, -1, keepdims=True)
    )


def iota(shape, dim):
    return lax.broadcasted_iota(jnp.int32, shape, dim)


def fill_perm(perm_ref, s, u, to_windows):
    for r0 in range(0, PATCHES, BLOCK):
        row = iota((BLOCK, 128), 0) + r0
        if to_windows:
            a = (row >> 2) & 3
            b = row & 3
            t = (4 * (row >> 5) + a + s) & (GRID_T - 1)
            f = (4 * ((row >> 4) & 1) + b + u) & (GRID_F - 1)
            source = t * GRID_F + f
        else:
            r = ((row >> 3) - s) & (GRID_T - 1)
            q = ((row & 7) - u) & (GRID_F - 1)
            source = (r >> 2) * 32 + (q >> 2) * 16 + (r & 3) * 4 + (q & 3)
        lane = iota((BLOCK, 128), 1)
        for c0 in range(0, PATCHES, 128):
            perm_ref[r0 : r0 + BLOCK, c0 : c0 + 128] = jnp.where(
                source == lane + c0, 1.0, 0.0
            ).astype(BF16)


def compact_code(rows):
    row = iota((rows, 128), 0)
    lane = iota((rows, 128), 1)
    return ((lane >> 4) - (row >> 4) - (lane >> 6)) & 3


def head_lanes(dtype):
    lane = iota((16, 128), 1) >> 5
    return [jnp.where(lane == hh, 1.0, 0.0).astype(dtype) for hh in range(4)]


def expand_rows(tile, g, lanes):
    parts = []
    for hh in range(4):
        half, ab = hh & 1, hh >> 1
        for slot in range(4):
            w = (slot - half - g - 2 * ab) % 4
            parts.append(tile[16 * w : 16 * w + 16, :] * lanes[hh])
    return jnp.concatenate(parts, axis=0)


def compact(code, s0, s1):
    return jnp.where(
        code == 0,
        s0[:, :128],
        jnp.where(code == 1, s1[:, :128], jnp.where(code == 2, s0[:, 128:], s1[:, 128:])),
    )


def lane_partner(x, k):
    lane = iota(x.shape, 1)
    return jnp.where((lane & k) == 0, pltpu.roll(x, 128 - k, 1), pltpu.roll(x, k, 1))


def group_max(x):
    for k in (1, 2, 4, 8):
        x = jnp.maximum(x, lane_partner(x, k))
    return x


def group_sum(x):
    for k in (1, 2, 4, 8):
        x = x + lane_partner(x, k)
    return x


def allowed_tile(block, s, u, count):
    row = iota((BLOCK, 128), 0)
    key = iota((BLOCK, 128), 1) & 15
    band = 4 * (2 * block + (row >> 5))
    side = 4 * ((row >> 4) & 1)
    r_i = band + ((row >> 2) & 3) + s
    q_i = side + (row & 3) + u
    r_j = band + (key >> 2) + s
    q_j = side + (key & 3) + u
    wrap_i = (r_i >> 6) * 2 + (q_i >> 3)
    wrap_j = (r_j >> 6) * 2 + (q_j >> 3)
    visible = ((r_j & (GRID_T - 1)) < count) | ((row & 15) == key)
    return (wrap_i == wrap_j) & visible


def attend_kernel(
    shift_ref, count_ref, tok_ref, w_ref, vec_ref, pos_ref,
    qkv_ref, prob_ref, ctx_ref,
    perm_ref, rows_ref, act_ref, score_ref, low_ref, ctxw_ref,
):
    width = tok_ref.shape[1]
    scale = (width // HEADS) ** (-0.5)
    clip = pl.program_id(0)
    s = shift_ref[clip, 0]
    u = shift_ref[clip, 1]
    count = count_ref[clip]
    fill_perm(perm_ref, s, u, True)
    rows_ref[...] = dot_nn(perm_ref[...], tok_ref[...])
    for r in range(0, PATCHES, ROWS):
        normed, _ = norm_stats(rows_ref[r : r + ROWS, :])
        act_ref[r : r + ROWS, :] = (normed * vec_ref[0:1, :] + vec_ref[1:2, :]).astype(BF16)
    for c in range(3):
        cols = slice(c * width, (c + 1) * width)
        out = dot_nn(act_ref[...], w_ref[:, cols])
        if c == 0:
            out = out + vec_ref[2:3, :]
        if c == 2:
            out = out + vec_ref[3:4, :]
        qkv_ref[:, cols] = out.astype(BF16)
    lanes = head_lanes(BF16)
    code = compact_code(BLOCK)
    for b in range(BLOCKS):
        rows = slice(b * BLOCK, (b + 1) * BLOCK)
        for p in range(2):
            parts = []
            for g in range(2):
                c0 = 128 * (2 * p + g)
                keys = expand_rows(qkv_ref[rows, width + c0 : width + c0 + 128], g, lanes)
                parts.append(dot_nt(qkv_ref[rows, c0 : c0 + 128], keys))
            score_ref[rows, 128 * p : 128 * p + 128] = compact(code, *parts)
    for b in range(BLOCKS):
        rows = slice(b * BLOCK, (b + 1) * BLOCK)
        allowed = allowed_tile(b, s, u, count)
        for p in range(2):
            cols = slice(128 * p, 128 * p + 128)
            logits = score_ref[rows, cols] * scale + pos_ref[:, cols]
            logits = jnp.where(allowed, logits, NEGATIVE)
            e = jnp.exp(logits - group_max(logits))
            prob = e * pl.reciprocal(group_sum(e))
            prob_ref[rows, cols] = prob
            low_ref[rows, cols] = prob.astype(BF16)
    spread = [jnp.where(code == e, 1.0, 0.0).astype(BF16) for e in range(4)]
    for b in range(BLOCKS):
        rows = slice(b * BLOCK, (b + 1) * BLOCK)
        for p in range(2):
            low = low_ref[rows, 128 * p : 128 * p + 128]
            for g in range(2):
                c0 = 128 * (2 * p + g)
                values = expand_rows(qkv_ref[rows, 2 * width + c0 : 2 * width + c0 + 128], g, lanes)
                wide = jnp.concatenate([low * spread[g], low * spread[2 + g]], axis=1)
                ctxw_ref[rows, c0 : c0 + 128] = dot_nn(wide, values).astype(BF16)
    fill_perm(perm_ref, s, u, False)
    ctx_ref[...] = dot_nn(perm_ref[...], ctxw_ref[...]).astype(BF16)


def mlp_kernel(
    tok_ref, ctx_ref, cot_ref, wp_ref, wu_ref, wd_ref, vec_ref, ub_ref,
    out_ref, gmid_ref, gctx_ref, gwp_ref, gwu_ref, gwd_ref, small_ref, gub_ref,
    accp_ref, accu_ref, accd_ref, mid_ref, act_ref, hid_ref, gg_ref, gl_ref, gh_ref, gact_ref, gb_ref,
):
    step = pl.program_id(0)
    tile = tok_ref.shape[0]
    ff = wu_ref.shape[1]
    chunk = 512

    @pl.when(step == 0)
    def _():
        accp_ref[...] = jnp.zeros_like(accp_ref)
        accu_ref[...] = jnp.zeros_like(accu_ref)
        accd_ref[...] = jnp.zeros_like(accd_ref)
        small_ref[...] = jnp.zeros_like(small_ref)
        gub_ref[...] = jnp.zeros_like(gub_ref)

    gain = vec_ref[0:1, :]
    bias = vec_ref[1:2, :]
    mid_ref[...] = dot_nn(ctx_ref[...], wp_ref[...])
    for r in range(0, tile, ROWS):
        rows = slice(r, r + ROWS)
        mid = mid_ref[rows, :] + tok_ref[rows, :].astype(F32) + vec_ref[2:3, :]
        mid_ref[rows, :] = mid
        normed, _ = norm_stats(mid)
        act_ref[rows, :] = (normed * gain + bias).astype(BF16)
    for c in range(0, ff, chunk):
        cols = slice(c, c + chunk)
        hid_ref[...] = dot_nn(act_ref[...], wu_ref[:, cols])
        gg_ref[...] = dot_nt(cot_ref[...], wd_ref[cols, :])
        for k in range(0, chunk, 128):
            lanes = slice(k, k + 128)
            total = jnp.zeros((1, 128), F32)
            for r in range(0, tile, 64):
                rows = slice(r, r + 64)
                h = hid_ref[rows, lanes] + ub_ref[0:1, c + k : c + k + 128]
                phi = 0.5 + 0.5 * lax.erf(h * (0.5**0.5))
                bell = jnp.exp(-0.5 * h * h) * 0.3989422804014327
                gl_ref[rows, lanes] = (h * phi).astype(BF16)
                g_hidden = (gg_ref[rows, lanes] * (phi + h * bell)).astype(BF16)
                gh_ref[rows, lanes] = g_hidden
                total = total + jnp.sum(g_hidden.astype(F32), 0, keepdims=True)
            gub_ref[0:1, c + k : c + k + 128] += total
        down = dot_nn(gl_ref[...], wd_ref[cols, :])
        back = dot_nt(gh_ref[...], wu_ref[:, cols])
        if c == 0:
            gb_ref[...] = down
            gact_ref[...] = back
        else:
            gb_ref[...] += down
            gact_ref[...] += back
        accd_ref[cols, :] += dot_tn(gl_ref[...], cot_ref[...])
        accu_ref[:, cols] += dot_tn(act_ref[...], gh_ref[...])
    sums = [jnp.zeros((1, tok_ref.shape[1]), F32) for _ in range(4)]
    for r in range(0, tile, ROWS):
        rows = slice(r, r + ROWS)
        mid = mid_ref[rows, :]
        out_ref[rows, :] = (mid + gb_ref[rows, :] + vec_ref[3:4, :]).astype(BF16)
        normed, inv = norm_stats(mid)
        g_act = gact_ref[rows, :]
        cot = cot_ref[rows, :].astype(F32)
        g_mid = cot + norm_back(g_act, normed, inv, gain)
        gmid_ref[rows, :] = g_mid
        g_branch = g_mid.astype(BF16)
        act_ref[rows, :] = g_branch
        sums[0] = sums[0] + jnp.sum(g_act * normed, 0, keepdims=True)
        sums[1] = sums[1] + jnp.sum(g_act, 0, keepdims=True)
        sums[2] = sums[2] + jnp.sum(g_branch.astype(F32), 0, keepdims=True)
        sums[3] = sums[3] + jnp.sum(cot, 0, keepdims=True)
    for i in range(4):
        small_ref[i : i + 1, :] += sums[i]
    gctx_ref[...] = dot_nt(act_ref[...], wp_ref[...]).astype(BF16)
    accp_ref[...] += dot_tn(ctx_ref[...], act_ref[...])

    @pl.when(step == pl.num_programs(0) - 1)
    def _():
        gwp_ref[...] = accp_ref[...].astype(BF16)
        gwu_ref[...] = accu_ref[...].astype(BF16)
        gwd_ref[...] = accd_ref[...].astype(BF16)


def attend_back_kernel(
    shift_ref, qkv_ref, prob_ref, gctx_ref, tok_ref, gmid_ref, w_ref, vec_ref,
    gtok_ref, gw_ref, small_ref, gpos_ref,
    acc_ref, perm_ref, do_ref, dp_ref, low_ref, gs_ref, lowt_ref, gst_ref, gqw_ref, gqn_ref, act_ref, gact_ref,
):
    width = tok_ref.shape[1]
    scale = (width // HEADS) ** (-0.5)
    clip = pl.program_id(0)
    s = shift_ref[clip, 0]
    u = shift_ref[clip, 1]

    @pl.when(clip == 0)
    def _():
        acc_ref[...] = jnp.zeros_like(acc_ref)
        small_ref[...] = jnp.zeros_like(small_ref)
        gpos_ref[...] = jnp.zeros_like(gpos_ref)

    fill_perm(perm_ref, s, u, True)
    do_ref[...] = dot_nn(perm_ref[...], gctx_ref[...]).astype(BF16)
    lanes = head_lanes(BF16)
    code = compact_code(BLOCK)
    for b in range(BLOCKS):
        rows = slice(b * BLOCK, (b + 1) * BLOCK)
        for p in range(2):
            parts = []
            for g in range(2):
                c0 = 128 * (2 * p + g)
                values = expand_rows(qkv_ref[rows, 2 * width + c0 : 2 * width + c0 + 128], g, lanes)
                parts.append(dot_nt(do_ref[rows, c0 : c0 + 128], values))
            dp_ref[rows, 128 * p : 128 * p + 128] = compact(code, *parts)
    for p in range(2):
        cols = slice(128 * p, 128 * p + 128)
        total = jnp.zeros((BLOCK, 128), F32)
        for b in range(BLOCKS):
            rows = slice(b * BLOCK, (b + 1) * BLOCK)
            prob = prob_ref[rows, cols]
            d_prob = dp_ref[rows, cols]
            g_scores = (prob * (d_prob - group_sum(prob * d_prob))).astype(BF16)
            gs_ref[rows, cols] = g_scores
            low_ref[rows, cols] = prob.astype(BF16)
            total = total + g_scores.astype(F32)
        gpos_ref[:, cols] += total
    spread = [jnp.where(code == e, 1.0, 0.0).astype(BF16) for e in range(4)]
    for b in range(BLOCKS):
        rows = slice(b * BLOCK, (b + 1) * BLOCK)
        for p in range(2):
            low = gs_ref[rows, 128 * p : 128 * p + 128]
            for g in range(2):
                c0 = 128 * (2 * p + g)
                keys = expand_rows(qkv_ref[rows, width + c0 : width + c0 + 128], g, lanes)
                wide = jnp.concatenate([low * spread[g], low * spread[2 + g]], axis=1)
                gqw_ref[rows, c0 : c0 + 128] = (dot_nn(wide, keys) * scale).astype(BF16)
    lowt_ref[...] = jnp.transpose(low_ref[...])
    gst_ref[...] = jnp.transpose(gs_ref[...])
    row_t = iota((BLOCK, 128), 0)
    lane_t = iota((BLOCK, 128), 1)
    code_t = ((row_t >> 4) - (lane_t >> 4)) & 3
    spread_t = [
        [jnp.where((code_t == d) & ((lane_t >> 6) == blk), 1.0, 0.0).astype(BF16) for d in range(4)]
        for blk in range(2)
    ]
    lane16 = iota((16, 128), 1) >> 5
    for source_ref, other_ref, other_at, out_at, factor in (
        (gst_ref, qkv_ref, 0, width, scale),
        (lowt_ref, do_ref, 0, 2 * width, 1.0),
    ):
        for two in range(BLOCKS // 2):
            places = slice(128 * two, 128 * two + 128)
            for p in range(2):
                halves = [source_ref[128 * p + 64 * h : 128 * p + 64 * h + 64, places] for h in range(2)]
                for g in range(2):
                    c0 = 128 * (2 * p + g)
                    parts = []
                    for blk in range(2):
                        for hh in range(4):
                            half, ab = hh & 1, hh >> 1
                            d = (g + 2 * ab + half) & 3
                            parts.append(halves[half] * spread_t[blk][d])
                    wide = dot_nn(
                        jnp.concatenate(parts, axis=0), other_ref[places, other_at + c0 : other_at + c0 + 128]
                    )
                    for blk in range(2):
                        for w in range(4):
                            pieces = []
                            for hh in range(4):
                                half, ab = hh & 1, hh >> 1
                                slot = (w + half + g + 2 * ab) & 3
                                at = 256 * blk + 64 * hh + 16 * slot
                                pieces.append(wide[at : at + 16, :])
                            total = jnp.where(
                                lane16 == 0,
                                pieces[0],
                                jnp.where(lane16 == 1, pieces[1], jnp.where(lane16 == 2, pieces[2], pieces[3])),
                            )
                            at = 128 * two + 64 * blk + 16 * w
                            gqw_ref[at : at + 16, out_at + c0 : out_at + c0 + 128] = (total * factor).astype(BF16)
    fill_perm(perm_ref, s, u, False)
    for c in range(3):
        cols = slice(c * width, (c + 1) * width)
        gqn_ref[:, cols] = dot_nn(perm_ref[...], gqw_ref[:, cols]).astype(BF16)
    for r in range(0, PATCHES, ROWS):
        rows = slice(r, r + ROWS)
        normed, _ = norm_stats(tok_ref[rows, :].astype(F32))
        act_ref[rows, :] = (normed * vec_ref[0:1, :] + vec_ref[1:2, :]).astype(BF16)
    gact_ref[...] = dot_nt(gqn_ref[...], w_ref[...])
    for c in range(3):
        cols = slice(c * width, (c + 1) * width)
        acc_ref[:, cols] += dot_tn(act_ref[...], gqn_ref[:, cols])
    sums = [jnp.zeros((1, width), F32) for _ in range(4)]
    for r in range(0, PATCHES, ROWS):
        rows = slice(r, r + ROWS)
        normed, inv = norm_stats(tok_ref[rows, :].astype(F32))
        g_act = gact_ref[rows, :]
        gtok_ref[rows, :] = gmid_ref[rows, :] + norm_back(g_act, normed, inv, vec_ref[0:1, :])
        sums[0] = sums[0] + jnp.sum(g_act * normed, 0, keepdims=True)
        sums[1] = sums[1] + jnp.sum(g_act, 0, keepdims=True)
        sums[2] = sums[2] + jnp.sum(gqn_ref[rows, :width].astype(F32), 0, keepdims=True)
        sums[3] = sums[3] + jnp.sum(gqn_ref[rows, 2 * width :].astype(F32), 0, keepdims=True)
    for i in range(4):
        small_ref[i : i + 1, :] += sums[i]

    @pl.when(clip == pl.num_programs(0) - 1)
    def _():
        gw_ref[...] = acc_ref[...].astype(BF16)


SMEM_SPEC = pl.BlockSpec(memory_space=pltpu.SMEM)


def rows_spec(rows, cols):
    return pl.BlockSpec((rows, cols), lambda i: (i, 0))


def whole_spec(shape):
    return pl.BlockSpec(shape, lambda i: (0,) * len(shape))


def struct(shape, dtype):
    return jax.ShapeDtypeStruct(shape, dtype)


def params():
    return pltpu.CompilerParams(vmem_limit_bytes=VMEM_BYTES, dimension_semantics=("arbitrary",))


def attend(shifts, counts, tokens, w_qkv, vec, pos):
    n, width = tokens.shape
    return pl.pallas_call(
        attend_kernel,
        grid=(n // PATCHES,),
        in_specs=[
            SMEM_SPEC, SMEM_SPEC, rows_spec(PATCHES, width),
            whole_spec(w_qkv.shape), whole_spec(vec.shape), whole_spec(pos.shape),
        ],
        out_specs=[rows_spec(PATCHES, 3 * width), rows_spec(PATCHES, 256), rows_spec(PATCHES, width)],
        out_shape=[struct((n, 3 * width), BF16), struct((n, 256), F32), struct((n, width), BF16)],
        scratch_shapes=[
            pltpu.VMEM((PATCHES, PATCHES), BF16),
            pltpu.VMEM((PATCHES, width), F32),
            pltpu.VMEM((PATCHES, width), BF16),
            pltpu.VMEM((PATCHES, 256), F32),
            pltpu.VMEM((PATCHES, 256), BF16),
            pltpu.VMEM((PATCHES, width), BF16),
        ],
        compiler_params=params(),
        name="attend",
    )(shifts, counts, tokens, w_qkv, vec, pos)


def mlp(tokens, ctx, cot, wp, wu, wd, vec, ub, tile=512):
    n, width = tokens.shape
    ff = wu.shape[1]
    return pl.pallas_call(
        mlp_kernel,
        grid=(n // tile,),
        in_specs=[rows_spec(tile, width)] * 3
        + [whole_spec(wp.shape), whole_spec(wu.shape), whole_spec(wd.shape), whole_spec(vec.shape), whole_spec(ub.shape)],
        out_specs=[rows_spec(tile, width)] * 3
        + [whole_spec(wp.shape), whole_spec(wu.shape), whole_spec(wd.shape), whole_spec((8, width)), whole_spec((8, ff))],
        out_shape=[
            struct((n, width), BF16), struct((n, width), F32), struct((n, width), BF16),
            struct(wp.shape, BF16), struct(wu.shape, BF16), struct(wd.shape, BF16),
            struct((8, width), F32), struct((8, ff), F32),
        ],
        scratch_shapes=[
            pltpu.VMEM((width, width), F32),
            pltpu.VMEM((width, ff), F32),
            pltpu.VMEM((ff, width), F32),
            pltpu.VMEM((tile, width), F32),
            pltpu.VMEM((tile, width), BF16),
            pltpu.VMEM((tile, 512), F32),
            pltpu.VMEM((tile, 512), F32),
            pltpu.VMEM((tile, 512), BF16),
            pltpu.VMEM((tile, 512), BF16),
            pltpu.VMEM((tile, width), F32),
            pltpu.VMEM((tile, width), F32),
        ],
        compiler_params=params(),
        name="mlp",
    )(tokens, ctx, cot, wp, wu, wd, vec, ub)


def attend_back(shifts, qkv, prob, gctx, tokens, gmid, w_qkv, vec):
    n, width = tokens.shape
    return pl.pallas_call(
        attend_back_kernel,
        grid=(n // PATCHES,),
        in_specs=[
            SMEM_SPEC, rows_spec(PATCHES, 3 * width), rows_spec(PATCHES, 256), rows_spec(PATCHES, width),
            rows_spec(PATCHES, width), rows_spec(PATCHES, width), whole_spec(w_qkv.shape), whole_spec(vec.shape),
        ],
        out_specs=[rows_spec(PATCHES, width), whole_spec(w_qkv.shape), whole_spec((8, width)), whole_spec((BLOCK, 256))],
        out_shape=[
            struct((n, width), F32), struct(w_qkv.shape, BF16), struct((8, width), F32), struct((BLOCK, 256), F32),
        ],
        scratch_shapes=[
            pltpu.VMEM(w_qkv.shape, F32),
            pltpu.VMEM((PATCHES, PATCHES), BF16),
            pltpu.VMEM((PATCHES, width), BF16),
            pltpu.VMEM((PATCHES, 256), F32),
            pltpu.VMEM((PATCHES, 256), BF16),
            pltpu.VMEM((PATCHES, 256), BF16),
            pltpu.VMEM((256, PATCHES), BF16),
            pltpu.VMEM((256, PATCHES), BF16),
            pltpu.VMEM((PATCHES, 3 * width), BF16),
            pltpu.VMEM((PATCHES, 3 * width), BF16),
            pltpu.VMEM((PATCHES, width), BF16),
            pltpu.VMEM((PATCHES, width), F32),
        ],
        compiler_params=params(),
        name="attend_back",
    )(shifts, qkv, prob, gctx, tokens, gmid, w_qkv, vec)


def offset_onehot():
    place = np.arange(PLACES)
    rows = place[:, None] // WIN - place[None, :] // WIN + WIN - 1
    cols = place[:, None] % WIN - place[None, :] % WIN + WIN - 1
    code = (rows * (2 * WIN - 1) + cols).reshape(-1)
    return (code[:, None] == np.arange((2 * WIN - 1) ** 2)[None, :]).astype(np.float32)


def head_spread():
    spread = np.zeros((HEADS * PLACES, 4, 2 * 128), np.float32)
    for w in range(4):
        for lane in range(256):
            p, half, slot, key = lane // 128, lane // 64 % 2, lane // 16 % 4, lane % 16
            e = (slot - w - half) % 4
            head = 8 * p + 4 * (e & 1) + 2 * (e >> 1) + half
            spread[head * PLACES + key, w, lane] = 1.0
    return spread.reshape(HEADS * PLACES, 1024)


def position_tile(table):
    by_pair = jnp.dot(jnp.asarray(offset_onehot()), table.astype(F32), precision=HIGH)
    by_row = by_pair.reshape(PLACES, PLACES, HEADS).transpose(0, 2, 1).reshape(PLACES, HEADS * PLACES)
    tiles = jnp.dot(by_row, jnp.asarray(head_spread()), precision=HIGH)
    return tiles.reshape(PLACES, 4, 256).transpose(1, 0, 2).reshape(BLOCK, 256)


def table_gradient(gpos):
    tiles = gpos.reshape(4, PLACES, 256).transpose(1, 0, 2).reshape(PLACES, 1024)
    by_row = jnp.dot(tiles, jnp.asarray(head_spread().T.copy()), precision=HIGH)
    by_pair = by_row.reshape(PLACES, HEADS, PLACES).transpose(0, 2, 1).reshape(PLACES * PLACES, HEADS)
    return jnp.dot(jnp.asarray(offset_onehot().T.copy()), by_pair, precision=HIGH)


def gather(x):
    return lax.all_gather(x, AXES, axis=0, tiled=True)


def scatter(x):
    return lax.psum_scatter(x, AXES, scatter_dimension=0, tiled=True)


def on_device(
    tokens, cotangent, counts, shifts, qkv_weight, proj_weight, up_weight, down_weight,
    first_gain, first_bias, second_gain, second_bias, query_bias, value_bias, proj_bias, up_bias, down_bias,
    rel_table,
):
    w_qkv = gather(qkv_weight)
    smalls = jnp.stack(
        [first_gain, first_bias, query_bias, value_bias, second_gain, second_bias, proj_bias, down_bias]
    )
    part = first_gain.shape[0]
    packed = jnp.concatenate([smalls.reshape(-1), up_bias])
    full = gather(packed[None]).astype(F32)
    vecs = full[:, : 8 * part].reshape(-1, 8, part).transpose(1, 0, 2).reshape(8, -1)
    ub = full[:, 8 * part :].reshape(1, -1)
    vec_one, vec_two = vecs[:4], vecs[4:]
    wp, wu, wd = gather(proj_weight), gather(up_weight), gather(down_weight)
    pos = position_tile(rel_table)
    qkv, prob, ctx = attend(shifts, counts, tokens, w_qkv, vec_one, pos)
    out, gmid, gctx, gwp, gwu, gwd, small_two, gub = mlp(tokens, ctx, cotangent, wp, wu, wd, vec_two, ub)
    gtok, gw_qkv, small_one, gpos = attend_back(shifts, qkv, prob, gctx, tokens, gmid, w_qkv, vec_one)
    table = lax.psum(table_gradient(gpos), AXES)
    ready = [scatter(x).astype(F32) for x in (gw_qkv, gwp, gwu, gwd)]
    rows = jnp.concatenate([small_one[:4], small_two[:4]])
    small = jnp.concatenate(
        [rows.reshape(8, -1, part).transpose(1, 0, 2).reshape(-1, 8 * part), gub[0].reshape(-1, up_bias.shape[0])], 1
    )
    mine = scatter(small)[0]
    grads = mine[: 8 * part].reshape(8, part)
    return (
        out, gtok, *ready,
        grads[0], grads[1], grads[4], grads[5], grads[2], grads[3], grads[6], mine[8 * part :], grads[7], table,
    )


def solution(mesh):
    sharded = P(AXES, None)
    line = P(AXES)
    in_specs = (sharded, sharded, line, sharded) + (sharded,) * 4 + (line,) * 9 + (P(),)
    out_specs = (sharded,) * 6 + (line,) * 9 + (P(),)
    return jax.shard_map(on_device, mesh=mesh, in_specs=in_specs, out_specs=out_specs, check_vma=False)
```

time: 739 us -> 747 us (1.011); the launches traced: 728 us -> 746 us
  waiting for transfers between devices: 46.4 us -> 453 us
  matrix products: 198 us -> 7.82 us
  local copies, waits for them, and re-layouts: 168 us -> 7.97 us
  Pallas kernels: 0 us -> 100 us
  other arithmetic: 93 us -> 6.47 us
  blocking collectives: 201 us -> 156 us
    reduce_scatter x8 -> x4, waiting for transfers between devices: 46.2 us -> 421 us  [scatter(): return lax.psum_scatter(x, AXES, scatter_dimension=0, tiled=True)]
    dot_general x20 -> x4, matrix products: 198 us -> 7.82 us  [the longest x1 3.75 us: table_gradient(): by_row = jnp.dot(tiles, jnp.asarray(head_spread().T.copy()), precision=HIGH)]
    pallas_call x0 -> x3, Pallas kernels: none -> 100 us  [the longest x1 45.7 us: mlp(): pl.pallas_call(mlp_kernel, grid=(n // tile,), in_specs=[rows_spec(tile, w...]
    gather x48 -> x0, local copies, waits for them, and re-layouts: 60.1 us -> none
    unnamed x143 -> x17, local copies, waits for them, and re-layouts: 42.4 us -> 1.62 us
    psum x1 -> x0, blocking collectives: 39.6 us -> none  [on_device(): table_total = lax.psum(table_term, ('dp', 'pair'))]
    reshape x3 -> x5, local copies, waits for them, and re-layouts: 36.7 us -> 1.01 us  [the longest x1 0.68 us: on_device(): ub = full[:, 8 * part:].reshape(1, -1)]
    convert_element_type x29 -> x4, other arithmetic: 35 us -> 5.79 us  [on_device(): ready = [scatter(x).astype(F32) for x in (gw_qkv, gwp, gwu, gwd)]]
  transfers between devices with their start and end apart: 11 -> 7, of which waited for: 2 -> 5; matrix products, arithmetic and copies ran while one was open for 48% -> 3% of each run, Pallas kernels for 0% -> 7%
where the time goes in v1:
time: 747 us; the launch traced here: 746 us
  waiting for transfers between devices  453 us (61%)
  blocking collectives  156 us (21%)
  Pallas kernels  100 us (13%)
  between operations  14.4 us (2%)
  local copies, waits for them, and re-layouts  7.97 us (1%)
  matrix products  7.82 us (1%)
    reduce_scatter x4, waiting for transfers between devices, scatter(): return lax.psum_scatter(x, AXES, scatter_dimension=0, tiled=True)  421 us
    unnamed x2, blocking collectives  82 us
    all_gather x1, blocking collectives, gather(): return lax.all_gather(x, AXES, axis=0, tiled=True)  74 us
    pallas_call x1, Pallas kernels, mlp(): pl.pallas_call(mlp_kernel, grid=(n // tile,), in_specs=[rows_spec(tile, w...  45.7 us
    pallas_call x1, Pallas kernels, attend_back(): pl.pallas_call(attend_back_kernel, grid=(n // PATCHES,), in_specs=[SMEM_S...  32 us
    all_gather x3, waiting for transfers between devices, gather(): return lax.all_gather(x, AXES, axis=0, tiled=True)  28.7 us
    pallas_call x1, Pallas kernels, attend(): pl.pallas_call(attend_kernel, grid=(n // PATCHES,), in_specs=[SMEM_SPEC,...  22.5 us
  transfers between devices with their start and end apart: 7, of which 5 were waited for; matrix products, arithmetic and copies ran while one was open for 3% of the time, Pallas kernels for 7%

profile of v1, /device:TPU:0, one launch (start us, length us, event | category | flops | bytes accessed | tf_op | source)
XLA Modules:
  0.0 746.5 jit_solution(1260882594085017743)
XLA Ops:
  7.3 0.7 all-gather.5.cloned.1.call-update
  8.0 0.7 all-gather.7.cloned.1.call-update
  8.7 0.7 all-gather.9.cloned.1.call-update
  9.4 0.0 reduce-scatter.8.cloned.1.call-start
  9.5 0.8 stack.35
  10.3 0.1 reshape.92
  10.4 0.7 pad_maximum_fusion.2
  11.0 0.2 dynamic-update-slice
  11.3 42.2 %all-reduce = bf16[6144]{0:T(1024)(128)(2,1)S(1)} all-reduce(bf16[6144]{0:T(1024)(128)(2,1)S(1)} %dynamic-update-slice), channel_id=2, replica_groups=mesh['dp'=16,'pair'=2] {'dp','pair'}, use_global_device_ids=true, to_apply=%add | all-reduce | flops 6144 | bytes 24576
  53.5 0.1 reshape.108
  53.6 0.1 copy.70
  53.7 0.1 copy.71
  53.8 0.7 slice.77.vec_ref
  54.5 1.3 copy.73.shift_ref
  55.8 1.1 fusion.1
  56.9 0.1 reshape.111
  57.0 0.1 copy.74
  57.1 0.7 slice.79.vec_ref
  57.8 0.7 reshape.97.ub_ref
  58.5 2.8 fusion.2
  61.3 74.0 %all_gather.17.wp_ref = bf16[512,512]{1,0:T(8,128)(2,1)} all-gather(bf16[16,512]{1,0:T(8,128)(2,1)S(1)} %copy-done.4), channel_id=1, replica_groups=mesh['dp'=16,'pair'=2] {'dp','pair'}, dimensions={0}, use_global_device_ids=true | all-gather | bytes 540672 | tf_op jit(solution)/shard_map/all_gather | solution.py:553
  135.4 22.5 %attend.1 = (bf16[2048,1536]{1,0:T(8,128)(2,1)}, f32[2048,256]{1,0:T(8,128)}, bf16[2048,512]{1,0:T(8,128)(2,1)}) custom-call(s32[4,2]{1,0:T(4,128)} %copy.73.shift_ref, s32[4]{0:T(128)} %count_ref.1, bf16[2048,512]{1,0:T(8,128)(2,1)} %tok_ref.5, bf16[512,1536]{1,0:T(8,128)(2,1)} %all-gather.5.cloned.1.call-done.w_ref, f32[4,512]{1,0:T(4,128)} %slice.77.vec_ref, ...), custom_call_target="tpu_custom_call" | custom-call | tf_op jit(solution)/shard_map/attend/pallas_call | solution.py:432
  157.9 28.7 %all-gather.9.cloned.1.call-done.wd_ref = bf16[2048,512]{1,0:T(8,128)(2,1)} async-done(((bf16[64,512]{1,0:T(8,128)(2,1)}), bf16[2048,512]{1,0:T(8,128)(2,1)}) %all-gather.9.cloned.1.call-update) | async-done | bytes 2097168 | tf_op jit(solution)/shard_map/all_gather | solution.py:553
  186.6 45.7 %mlp.1 = (bf16[2048,512]{1,0:T(8,128)(2,1)}, f32[2048,512]{1,0:T(8,128)}, bf16[2048,512]{1,0:T(8,128)(2,1)}, bf16[512,512]{1,0:T(8,128)(2,1)}, bf16[512,2048]{1,...) custom-call(bf16[2048,512]{1,0:T(8,128)(2,1)} %tok_ref.5, ...), custom_call_target="tpu_custom_call" | custom-call | tf_op jit(solution)/shard_map/mlp/pallas_call | solution.py:457
  232.3 0.0 reduce-scatter.6.cloned.1.call-start
  232.4 32.0 %attend_back.1 = (f32[2048,512]{1,0:T(8,128)}, bf16[512,1536]{1,0:T(8,128)(2,1)}, f32[8,512]{1,0:T(8,128)}, f32[64,256]{1,0:T(8,128)}) custom-call(s32[4,2]{1,0:T(4,128)} %copy.73.shift_ref, bf16[2048,1536]{1,0:T(8,128)(2,1)} %get-tuple-element.33.qkv_ref, f32[2048,256]{1,0:T(8,128)} %get-tuple-element.34.prob_ref, ...), custom_call_target="tpu_custom_call" | custom-call | tf_op jit(solution)/shard_map/attend_back/pallas_call | solution.py:489
  264.4 0.0 reduce-scatter.10.cloned.1.call-start
  264.5 0.5 reduce-scatter.10.cloned.1.call-update
  265.0 0.7 reduce-scatter.12.cloned.1.call-update
  265.8 0.1 reshape.98
  265.9 0.1 copy.76
  266.0 0.9 slice_reduce_fusion
  266.8 0.1 reshape_squeeze.3
  266.9 0.1 copy.77
  267.1 3.8 convolution_bitcast_fusion
  270.9 0.1 reshape.102
  271.0 0.1 fusion.3
  271.2 39.8 %all-reduce.2 = (f32[32,192]{0,1:T(8,128)S(1)}, f32[49,16]{0,1:T(8,128)}) all-reduce(f32[32,192]{0,1:T(8,128)S(1)} %pad_maximum_fusion, f32[49,16]{0,1:T(8,128)S(1)} %fusion.3), channel_id=7, replica_groups=mesh['dp'=16,'pair'=2] {'dp','pair'}, use_global_device_ids=true, to_apply=%region_4.0.clone | all-reduce | flops 6928 | bytes 55424
  311.0 0.7 dynamic-slice_reduce_fusion
  311.6 0.8 dynamic-slice_reduce_fusion.1
  312.5 53.0 %reduce-scatter.8.cloned.1.call-done = bf16[16,512]{1,0:T(8,128)(2,1)} async-done(((bf16[512,512]{1,0:T(8,128)(2,1)}), bf16[16,512]{1,0:T(8,128)(2,1)}) %reduce-scatter.8.cloned.1.call-update) | async-done | bytes 16400 | tf_op jit(solution)/shard_map/reduce_scatter | solution.py:557
  365.5 1.3 convert_element_type.18
  366.8 97.6 %reduce-scatter.6.cloned.1.call-done = bf16[16,1536]{1,0:T(8,128)(2,1)} async-done(((bf16[512,1536]{1,0:T(8,128)(2,1)}), bf16[16,1536]{1,0:T(8,128)(2,1)}) %reduce-scatter.6.cloned.1.call-update) | async-done | bytes 49168 | tf_op jit(solution)/shard_map/reduce_scatter | solution.py:557
  464.4 1.4 convert_element_type.17
  465.8 136.7 %reduce-scatter.10.cloned.1.call-done = bf16[16,2048]{1,0:T(8,128)(2,1)} async-done(((bf16[512,2048]{1,0:T(8,128)(2,1)}), bf16[16,2048]{1,0:T(8,128)(2,1)}) %reduce-scatter.10.cloned.1.call-update) | async-done | bytes 65552 | tf_op jit(solution)/shard_map/reduce_scatter | solution.py:557
  602.5 1.5 convert_element_type.19
  604.0 134.1 %reduce-scatter.12.cloned.1.call-done = bf16[64,512]{1,0:T(8,128)(2,1)} async-done(((bf16[2048,512]{1,0:T(8,128)(2,1)}), bf16[64,512]{1,0:T(8,128)(2,1)}) %reduce-scatter.12.cloned.1.call-update) | async-done | bytes 65552 | tf_op jit(solution)/shard_map/reduce_scatter | solution.py:557
  738.1 1.5 convert_element_type.20
  (32 shorter events, 0.4 us)
Async XLA Ops:
  7.2 48.6 %copy-start = (bf16[49,16]{0,1:T(8,128)(2,1)S(1)}, bf16[49,16]{0,1:T(8,128)(2,1)}, u32[]{:S(2)}) copy-start(bf16[49,16]{0,1:T(8,128)(2,1)} %param.39) | copy-start | bytes 4708
  7.2 54.1 %copy-start.4 = (bf16[16,512]{1,0:T(8,128)(2,1)S(1)}, bf16[16,512]{1,0:T(8,128)(2,1)}, u32[]{:S(2)}) copy-start(bf16[16,512]{1,0:T(8,128)(2,1)} %param.27) | copy-start | bytes 49156
  7.2 128.2 %all-gather.5.cloned.1.call-start = ((), (), s32[]{:S(2)}) async-start(), calls=%async_computation.4 | async-start | bytes 1622016 | tf_op jit(solution)/shard_map/all_gather | solution.py:553
  7.9 149.9 %all-gather.7.cloned.1.call-start = ((), (), s32[]{:S(2)}) async-start(), calls=%async_computation.5 | async-start | bytes 2162688 | tf_op jit(solution)/shard_map/all_gather | solution.py:553
  8.7 177.9 %all-gather.9.cloned.1.call-start = ((), (), s32[]{:S(2)}) async-start(), calls=%async_computation.6 | async-start | bytes 2162688 | tf_op jit(solution)/shard_map/all_gather | solution.py:553
  9.4 356.1 %reduce-scatter.8.cloned.1.call-start = ((), (), s32[]{:S(2)}) async-start(), calls=%async_computation.8 | async-start | bytes 540672 | tf_op jit(solution)/shard_map/reduce_scatter | solution.py:557
  232.3 232.0 %reduce-scatter.6.cloned.1.call-start = ((), (), s32[]{:S(2)}) async-start(), calls=%async_computation.7 | async-start | bytes 1622016 | tf_op jit(solution)/shard_map/reduce_scatter | solution.py:557
  264.4 338.1 %reduce-scatter.10.cloned.1.call-start = ((), (), s32[]{:S(2)}) async-start(), calls=%async_computation.9 | async-start | bytes 2162688 | tf_op jit(solution)/shard_map/reduce_scatter | solution.py:557
  264.4 1.3 copy-start.6
  264.4 1.3 copy-start.5
  264.5 2.5 copy-start.2
  264.5 2.6 copy-start.1
  265.0 473.2 %reduce-scatter.12.cloned.1.call-start = ((), (), s32[]{:S(2)}) async-start(), calls=%async_computation.10 | async-start | bytes 2162688 | tf_op jit(solution)/shard_map/reduce_scatter | solution.py:557
  265.0 6.0 copy-start.3
Sparse Core Ops, SparseCore 0:
  10.9 57.7 all-gather.4
  71.9 55.9 all-gather.6
  130.9 55.6 all-gather.8
  232.5 132.9 reduce-scatter.7
  371.4 92.9 reduce-scatter.5
  466.6 135.8 reduce-scatter.9
  604.8 133.3 reduce-scatter.11
